TPU v7x, 128 devices: a whole 4x4x4 slice. The times are simulated.
128 devices in a mesh: seq: 32 (over z, y, x_hi), tp: 4 (over x_lo, core).
Axes of the slice: x: 4 (x_hi: 2, x_lo: 2; x = x_hi * 2 + x_lo), y: 4, z: 4, core: 2. Of those that a mesh axis runs over, the one named last changes fastest.
Arguments:
- residual: bfloat16 [16384, 4096], P(('seq', 'tp')), may hold values from -6 to 6
- norm_gain: float32 [4096], replicated, may hold values from 0.1 to 1.9
- query_weight: bfloat16 [4096, 2048], P('seq', 'tp'), may hold values from -0.109375 to 0.109375
- keyval_weight: bfloat16 [896, 2, 2048], P('seq', None, 'tp'), may hold values from -0.2338536 to 0.2338536
- output_weight: bfloat16 [4096, 2048], P('seq', 'tp'), may hold values from -0.125 to 0.125
- neighbours: bfloat16 [512, 128, 896], P(('seq', 'tp')), may hold values from -6 to 6
- cotangent: bfloat16 [16384, 4096], P(('seq', 'tp')), may hold values from -6 to 6
Outputs:
- layer_output: bfloat16 [16384, 4096], P(('seq', 'tp'))
- residual_grad: bfloat16 [16384, 4096], P(('seq', 'tp'))
- neighbour_grad: bfloat16 [512, 128, 896], P(('seq', 'tp'))
- gain_grad: float32 [4096], replicated
- query_grad: float32 [4096, 2048], P('seq', 'tp')
- keyval_grad: float32 [896, 2, 2048], P('seq', None, 'tp')
- output_grad: float32 [4096, 2048], P('seq', 'tp')
All inputs are finite; a program needn't handle non-finite values.
Results may differ from a plain program's by a relative error of at most 0.03.
Values may be sent and summed in bfloat16 or wider, within the bound.
No kernel may reach another device: no remote copies, remote signals or barrier semaphores. Data moves between devices by JAX's collectives and lax.ppermute only.
A program may use at most 192 MiB of HBM per device.

v0:
```python
import math

import jax
import jax.numpy as jnp
from jax import lax
from jax.sharding import PartitionSpec as P

HEAD_DIM = 128
SPAN = 64
K_NB = 2
R = 128
LENGTH = 2048


EPSILON = 1e-06


def passed_along(value, axis, steps):
    count = lax.axis_size(axis)
    initial, last = (max(0, -steps), min(count, count - steps))
    return lax.ppermute(value, axis, [(source, source + steps) for source in range(initial, last)])


def span_forward(query, keys_prev, keys_cur, values_prev, values_cur, prev_rows, usable):
    factor = 1.0 / math.sqrt(query.shape[-1])
    prev_mask = prev_rows[None, None, :, None]
    score_prev = jnp.einsum("cqhd,ckhd->chqk", query, keys_prev, preferred_element_type=jnp.float32)
    score_cur = jnp.einsum("cqhd,ckhd->chqk", query, keys_cur, preferred_element_type=jnp.float32)
    scores = jnp.where(prev_mask, score_prev, score_cur) * factor
    row_peak = jnp.max(scores, axis=-1, keepdims=True)
    exponent = jnp.exp(scores - row_peak)
    probabilities = exponent / jnp.sum(exponent, axis=-1, keepdims=True)
    weights = probabilities.astype(jnp.bfloat16)
    zero_weight = jnp.zeros_like(weights)
    weights_prev = jnp.where(prev_mask, weights, zero_weight)
    weights_cur = jnp.where(prev_mask, zero_weight, weights)
    attended = jnp.einsum(
        "chqk,ckhd->cqhd", weights_prev, values_prev, preferred_element_type=jnp.float32
    )
    attended = attended + jnp.einsum(
        "chqk,ckhd->cqhd", weights_cur, values_cur, preferred_element_type=jnp.float32
    )
    attended = attended * usable[:, :, None, None]
    return (attended, probabilities, weights_prev, weights_cur)


def span_backward(
    upstream,
    query,
    keys_prev,
    keys_cur,
    values_prev,
    values_cur,
    prev_rows,
    usable,
    probabilities,
    weights_prev,
    weights_cur,
):
    factor = 1.0 / math.sqrt(query.shape[-1])
    prev_mask = prev_rows[None, None, :, None]
    masked_grad = jnp.where(usable[:, :, None, None] > 0, upstream, jnp.zeros_like(upstream))
    grad_prev = jnp.einsum(
        "cqhd,ckhd->chqk", masked_grad, values_prev, preferred_element_type=jnp.float32
    )
    grad_cur = jnp.einsum(
        "cqhd,ckhd->chqk", masked_grad, values_cur, preferred_element_type=jnp.float32
    )
    weight_grad = jnp.where(prev_mask, grad_prev, grad_cur)
    inner = jnp.sum(weight_grad * probabilities, axis=-1, keepdims=True)
    score_grad = (probabilities * (weight_grad - inner) * factor).astype(jnp.bfloat16)
    zero_score = jnp.zeros_like(score_grad)
    score_prev_grad = jnp.where(prev_mask, score_grad, zero_score)
    score_cur_grad = jnp.where(prev_mask, zero_score, score_grad)
    query_grad = jnp.einsum(
        "chqk,ckhd->cqhd", score_prev_grad, keys_prev, preferred_element_type=jnp.float32
    )
    query_grad = query_grad + jnp.einsum(
        "chqk,ckhd->cqhd", score_cur_grad, keys_cur, preferred_element_type=jnp.float32
    )
    keys_prev_grad = jnp.einsum(
        "chqk,cqhd->ckhd", score_prev_grad, query, preferred_element_type=jnp.float32
    )
    keys_cur_grad = jnp.einsum(
        "chqk,cqhd->ckhd", score_cur_grad, query, preferred_element_type=jnp.float32
    )
    values_prev_grad = jnp.einsum(
        "chqk,cqhd->ckhd", weights_prev, masked_grad, preferred_element_type=jnp.float32
    )
    values_cur_grad = jnp.einsum(
        "chqk,cqhd->ckhd", weights_cur, masked_grad, preferred_element_type=jnp.float32
    )
    return (query_grad, keys_prev_grad, keys_cur_grad, values_prev_grad, values_cur_grad)


def per_device(
    residual, norm_gain, query_weight, keyval_weight, output_weight, neighbours, cotangent
):
    residual_wide = residual.astype(jnp.float32)
    mean_square = jnp.mean(residual_wide * residual_wide, axis=-1, keepdims=True)
    inverse_rms = lax.rsqrt(mean_square + EPSILON)
    scaled = residual_wide * inverse_rms
    normed = (scaled * norm_gain).astype(jnp.bfloat16)
    group_normed, group_neighbours = (
        lax.all_gather(normed, "tp", axis=0, tiled=True),
        lax.all_gather(neighbours, "tp", axis=0, tiled=True),
    )
    full_query, full_output, full_keyval = (
        lax.all_gather(query_weight, "seq", axis=0, tiled=True),
        lax.all_gather(output_weight, "seq", axis=0, tiled=True),
        lax.all_gather(keyval_weight, "seq", axis=0, tiled=True),
    )
    local_width = query_weight.shape[1]
    heads_here = local_width // HEAD_DIM
    group_tokens = group_normed.shape[0]
    span_count = group_tokens // SPAN
    group_count = group_neighbours.shape[0]
    query = jnp.dot(group_normed, full_query, preferred_element_type=jnp.float32).astype(
        jnp.bfloat16
    )
    keyvals = jnp.einsum(
        "nre,etc->nrtc", group_neighbours, full_keyval, preferred_element_type=jnp.float32
    ).astype(jnp.bfloat16)
    arrived = passed_along(keyvals[group_count - K_NB :], "seq", 1)
    prev_flat = jnp.concatenate([arrived, keyvals[: group_count - K_NB]], axis=0)
    span_keyvals = keyvals.reshape(span_count, K_NB * R, 2, heads_here, HEAD_DIM)
    prev_keyvals = prev_flat.reshape(span_count, K_NB * R, 2, heads_here, HEAD_DIM)
    span_query = query.reshape(span_count, SPAN, heads_here, HEAD_DIM)
    prev_rows = jnp.arange(SPAN) < SPAN - 1
    positions = lax.axis_index("seq") * group_tokens + jnp.arange(group_tokens)
    usable = (positions % LENGTH >= SPAN - 1).astype(jnp.float32).reshape(span_count, SPAN)
    attended_wide, probabilities, weights_prev, weights_cur = span_forward(
        span_query,
        prev_keyvals[:, :, 0],
        span_keyvals[:, :, 0],
        prev_keyvals[:, :, 1],
        span_keyvals[:, :, 1],
        prev_rows,
        usable,
    )
    attended = attended_wide.astype(jnp.bfloat16).reshape(group_tokens, local_width)
    rows_part = attended
    mixed = lax.psum_scatter(
        jnp.einsum("th,dh->td", rows_part, full_output, preferred_element_type=jnp.float32).astype(
            jnp.bfloat16
        ),
        "tp",
        scatter_dimension=0,
        tiled=True,
    ).astype(jnp.float32)
    layer_output = (residual_wide + mixed).astype(jnp.bfloat16)
    group_cotangent = lax.all_gather(cotangent, "tp", axis=0, tiled=True)
    attended_grad = jnp.dot(
        group_cotangent, full_output, preferred_element_type=jnp.float32
    ).astype(jnp.bfloat16)
    query_grad_wide, keys_prev_grad, keys_cur_grad, values_prev_grad, values_cur_grad = (
        span_backward(
            attended_grad.reshape(span_count, SPAN, heads_here, HEAD_DIM),
            span_query,
            prev_keyvals[:, :, 0],
            span_keyvals[:, :, 0],
            prev_keyvals[:, :, 1],
            span_keyvals[:, :, 1],
            prev_rows,
            usable,
            probabilities,
            weights_prev,
            weights_cur,
        )
    )
    current_grad = jnp.stack([keys_cur_grad, values_cur_grad], axis=2).reshape(
        group_count, R, 2, local_width
    )
    previous_grad = jnp.stack([keys_prev_grad, values_prev_grad], axis=2).reshape(
        group_count, R, 2, local_width
    )
    returned = passed_along(previous_grad[:K_NB].astype(jnp.bfloat16), "seq", -1).astype(
        jnp.float32
    )
    keyval_back = (current_grad + jnp.concatenate([previous_grad[K_NB:], returned], axis=0)).astype(
        jnp.bfloat16
    )
    query_back = query_grad_wide.astype(jnp.bfloat16).reshape(group_tokens, local_width)
    rows_part = query_back
    feature_grad = lax.psum_scatter(
        jnp.einsum("th,dh->td", rows_part, full_query, preferred_element_type=jnp.float32).astype(
            jnp.bfloat16
        ),
        "tp",
        scatter_dimension=0,
        tiled=True,
    ).astype(jnp.float32)
    gained = feature_grad * norm_gain
    residual_grad = (
        inverse_rms * (gained - scaled * jnp.mean(gained * scaled, axis=-1, keepdims=True))
        + cotangent.astype(jnp.float32)
    ).astype(jnp.bfloat16)
    gain_grad = lax.psum(jnp.sum(feature_grad * scaled, axis=0), ("seq", "tp"))
    query_part = jnp.einsum(
        "td,th->dh", group_normed, query_back, preferred_element_type=jnp.float32
    )
    output_part = jnp.einsum(
        "td,th->dh", group_cotangent, attended, preferred_element_type=jnp.float32
    )
    projection_grads = lax.psum_scatter(
        jnp.stack([query_part, output_part], axis=1).astype(jnp.bfloat16),
        "seq",
        scatter_dimension=0,
        tiled=True,
    ).astype(jnp.float32)
    query_grad = projection_grads[:, 0]
    output_grad = projection_grads[:, 1]
    keyval_grad = lax.psum_scatter(
        jnp.einsum(
            "nre,nrtc->etc", group_neighbours, keyval_back, preferred_element_type=jnp.float32
        ).astype(jnp.bfloat16),
        "seq",
        scatter_dimension=0,
        tiled=True,
    ).astype(jnp.float32)
    rows_part = keyval_back
    neighbour_grad = lax.psum_scatter(
        jnp.einsum(
            "nrtc,etc->nre", rows_part, full_keyval, preferred_element_type=jnp.float32
        ).astype(jnp.bfloat16),
        "tp",
        scatter_dimension=0,
        tiled=True,
    )
    return (
        layer_output,
        residual_grad,
        neighbour_grad,
        gain_grad,
        query_grad,
        keyval_grad,
        output_grad,
    )


def solution(mesh):
    in_specs = (
        P(("seq", "tp"), None),
        P(),
        P("seq", "tp"),
        P("seq", None, "tp"),
        P("seq", "tp"),
        P(("seq", "tp"), None, None),
        P(("seq", "tp"), None),
    )
    out_specs = (
        P(("seq", "tp"), None),
        P(("seq", "tp"), None),
        P(("seq", "tp"), None, None),
        P(),
        P("seq", "tp"),
        P("seq", None, "tp"),
        P("seq", "tp"),
    )
    return jax.shard_map(
        per_device, mesh=mesh, in_specs=in_specs, out_specs=out_specs, check_vma=False
    )
```

profile of v0, /device:TPU:0, one launch (start us, length us, event | category | flops | bytes accessed | tf_op | source)
XLA Modules:
  0.0 1263.0 jit_solution(18150771448719188434)
XLA Ops:
  12.8 70.9 %all-gather.9.cloned.1.call-done = bf16[896,2,512]{2,1,0:T(2,128)(2,1)} async-done(((bf16[28,2,512]{2,1,0:T(2,128)(2,1)}), bf16[896,2,512]{2,1,0:T(2,128)(2,1)}) %all-gather.9.cloned.1.call-update) | async-done | bytes 1835024 | tf_op jit(solution)/shard_map/all_gather | solution.py:111
  83.7 41.3 %all-gather.7.cloned.1.call-done = bf16[16,128,896]{2,1,0:T(8,128)(2,1)} async-done(((bf16[4,128,896]{2,1,0:T(8,128)(2,1)}), bf16[16,128,896]{2,1,0:T(8,128)(2,1)}) %all-gather.7.cloned.1.call-update) | async-done | bytes 3670032 | tf_op jit(solution)/shard_map/all_gather | solution.py:106
  125.0 7.1 fusion.17
  134.1 4.6 collective-permute-start
  138.8 4.5 slice.51
  143.3 8.0 copy.51
  151.3 7.1 reshape.91
  158.5 3.8 fusion.134
  168.7 4.4 pad_maximum_fusion.1
  173.1 8.0 copy.47
  181.0 7.1 reshape.89
  188.1 4.6 fusion.133
  192.7 4.5 copy.77
  197.2 5.0 copy.75
  202.2 67.2 %all-gather.15.cloned.1.call-done = bf16[4096,512]{1,0:T(8,128)(2,1)} async-done(((bf16[128,512]{1,0:T(8,128)(2,1)}), bf16[4096,512]{1,0:T(8,128)(2,1)}) %all-gather.15.cloned.1.call-update) | async-done | bytes 4194320 | tf_op jit(solution)/shard_map/all_gather | solution.py:110
  269.4 5.8 convolution_convert_fusion.4
  275.3 41.0 %all-gather.11.cloned.1.call-done = bf16[512,4096]{1,0:T(8,128)(2,1)} async-done(((bf16[128,4096]{1,0:T(8,128)(2,1)}), bf16[512,4096]{1,0:T(8,128)(2,1)}) %all-gather.11.cloned.1.call-update) | async-done | bytes 4194320 | tf_op jit(solution)/shard_map/all_gather | solution.py:105
  316.3 84.9 %all-gather.13.cloned.1.call-done = bf16[4096,512]{1,0:T(8,128)(2,1)} async-done(((bf16[128,512]{1,0:T(8,128)(2,1)}), bf16[4096,512]{1,0:T(8,128)(2,1)}) %all-gather.13.cloned.1.call-update) | async-done | bytes 4194320 | tf_op jit(solution)/shard_map/all_gather | solution.py:109
  401.1 6.6 convolution_convert_fusion.5
  419.2 17.1 %convolution_bitcast_fusion.1 = f32[8,256,1,4,128]{1,4,3,0,2:T(8,128)} fusion(pred[64]{0:T(512)(128)(4,1)S(1)} %iota_compare_fusion, f32[8,4,64,256]{3,2,1,0:T(8,128)} %fusion.57, bf16[8,64,4,128]{3,2,1,0:T(4,128)(2,1)S(1)} %reshape.90, f32[8,4,64,256]{3,2,1,0:T(8,128)} %get-tuple-element.32, f32[8,4,64]{2,1,0:T(4,128)S(1)} %get-tuple-element.31), kind=kOutput, calls=%fused_computation.35 | convolution fusion | flops 138414336 | bytes 8921152 | tf_op jit(solution)/shard_map/chqk,cqhd->ckhd/dot_general | solution.py:81
  436.3 17.2 %convolution_bitcast_fusion.3 = f32[8,256,4,128]{1,3,2,0:T(8,128)} fusion(pred[64]{0:T(512)(128)(4,1)S(1)} %iota_compare_fusion, f32[8,4,64,256]{3,2,1,0:T(8,128)} %fusion.57, bf16[8,64,4,128]{3,2,1,0:T(4,128)(2,1)S(1)} %reshape.90, f32[8,4,64,256]{3,2,1,0:T(8,128)} %get-tuple-element.32, f32[8,4,64]{2,1,0:T(4,128)S(1)} %get-tuple-element.31), kind=kOutput, calls=%fused_computation.37 | convolution fusion | flops 138414336 | bytes 8921152 | tf_op jit(solution)/shard_map/chqk,cqhd->ckhd/dot_general | solution.py:84
  453.5 8.5 convolution_bitcast_fusion
  462.0 6.6 copy.59
  468.6 4.8 stack.30
  476.8 3.6 fusion.3
  480.4 7.4 copy.73
  487.8 9.1 reshape.100
  496.9 8.5 convolution_bitcast_fusion.2
  505.4 6.6 copy.60
  512.0 4.7 stack.31
  517.1 6.8 fusion.2
  525.8 5.9 fusion.50
  531.7 5.5 copy.68
  537.3 16.2 %fusion.35 = f32[8,4,128,64]{2,3,1,0:T(8,128)} fusion(bf16[8,256,1,4,128]{4,1,3,0,2:T(8,128)(2,1)} %copy.76, pred[64]{0:T(512)(128)(4,1)S(1)} %iota_compare_fusion, f32[8,4,64,256]{3,2,1,0:T(8,128)} %fusion.57, f32[8,4,64,256]{3,2,1,0:T(8,128)} %get-tuple-element.32, f32[8,4,64]{2,1,0:T(4,128)S(1)} %get-tuple-element.31), kind=kOutput, calls=%fused_computation.50 | convolution fusion | flops 138414336 | bytes 7348288 | tf_op jit(solution)/shard_map/chqk,ckhd->cqhd/dot_general | solution.py:78
  553.5 15.4 %fusion.79 = bf16[8,64,4,128]{3,1,2,0:T(8,128)(2,1)S(1)} fusion(f32[8,4,128,64]{2,3,1,0:T(8,128)} %fusion.35, bf16[8,256,1,4,128]{4,1,3,0,2:T(8,128)(2,1)} %copy.75, pred[64]{0:T(512)(128)(4,1)S(1)} %iota_compare_fusion, f32[8,4,64,256]{3,2,1,0:T(8,128)} %fusion.57, f32[8,4,64,256]{3,2,1,0:T(8,128)} %get-tuple-element.32, f32[8,4,64]{2,1,0:T(4,128)S(1)} %get-tuple-element.31), kind=kOutput, calls=%fused_computation.80 | convolution fusion | flops 138938624 | bytes 7872576 | tf_op jit(solution)/shard_map/chqk,ckhd->cqhd/dot_general | solution.py:75
  569.4 6.5 convolution_convert_fusion.2
  576.4 6.9 fusion.33
  583.3 7.0 fusion.82
  590.8 6.6 convolution_convert_fusion.3
  597.6 4.7 fusion.4
  602.3 4.4 fusion.5
  606.7 6.2 pad_maximum_fusion
  614.4 8.8 bitcast_convert_fusion
  625.0 272.4 %all-reduce.3.cloned.1.call-done = bf16[896,2,512]{2,1,0:T(2,128)(2,1)} async-done(((bf16[896,2,512]{2,1,0:T(2,128)(2,1)}), bf16[896,2,512]{2,1,0:T(2,128)(2,1)}) %all-reduce.3.cloned.1.call-update) | async-done | bytes 1835024
  898.9 46.8 %reduce-scatter.7.cloned.1.call-done = bf16[128,4096]{1,0:T(8,128)(2,1)} async-done(((bf16[512,4096]{1,0:T(8,128)(2,1)}), bf16[128,4096]{1,0:T(8,128)(2,1)}) %reduce-scatter.7.cloned.1.call-update) | async-done | bytes 1048592 | tf_op jit(solution)/shard_map/reduce_scatter | solution.py:185
  947.9 74.8 %psum.7 = f32[4096]{0:T(1024)} all-reduce(f32[4096]{0:T(1024)S(1)} %get-tuple-element.21), channel_id=1, replica_groups=mesh['seq'=32,'tp'=4] {'seq','tp'}, use_global_device_ids=true, to_apply=%region_9.10 | all-reduce | flops 4096 | bytes 32768 | tf_op jit(solution)/shard_map/psum | solution.py:198
  1026.3 188.6 %reduce-scatter.11.cloned.1.call-done = bf16[128,2,512]{2,0,1:T(8,128)(2,1)} async-done(((bf16[4096,2,512]{2,0,1:T(8,128)(2,1)}), bf16[128,2,512]{2,0,1:T(8,128)(2,1)}) %reduce-scatter.11.cloned.1.call-update) | async-done | bytes 262160 | tf_op jit(solution)/shard_map/reduce_scatter | solution.py:205
  1216.7 39.6 %reduce-scatter.9.cloned.1.call-done = bf16[4,128,896]{2,1,0:T(8,128)(2,1)} async-done(((bf16[16,128,896]{2,1,0:T(8,128)(2,1)}), bf16[4,128,896]{2,1,0:T(8,128)(2,1)}) %reduce-scatter.9.cloned.1.call-update) | async-done | bytes 917520 | tf_op jit(solution)/shard_map/reduce_scatter | solution.py:222
  (89 shorter events, 44.5 us)
Async XLA Ops:
  7.2 2.9 copy-start.1
  7.2 3.7 copy-start.9
  7.2 76.5 %all-gather.9.cloned.1.call-start = ((), (), s32[]{:S(2)}) async-start(), calls=%async_computation.5 | async-start | bytes 1892352 | tf_op jit(solution)/shard_map/all_gather | solution.py:111
  7.9 117.1 %all-gather.7.cloned.1.call-start = ((), (), s32[]{:S(2)}) async-start(), calls=%async_computation.4 | async-start | bytes 4587520 | tf_op jit(solution)/shard_map/all_gather | solution.py:106
  8.7 193.5 %all-gather.17.cloned.1.call-start = ((), (), s32[]{:S(2)}) async-start(), calls=%async_computation.10 | async-start | bytes 5242880 | tf_op jit(solution)/shard_map/all_gather | solution.py:152
  9.4 259.9 %all-gather.15.cloned.1.call-start = ((), (), s32[]{:S(2)}) async-start(), calls=%async_computation.8 | async-start | bytes 4325376 | tf_op jit(solution)/shard_map/all_gather | solution.py:110
  10.0 306.3 %all-gather.11.cloned.1.call-start = ((), (), s32[]{:S(2)}) async-start(), calls=%async_computation.6 | async-start | bytes 5242880 | tf_op jit(solution)/shard_map/all_gather | solution.py:105
  10.3 0.5 copy-start.11
  12.2 389.0 %all-gather.13.cloned.1.call-start = ((), (), s32[]{:S(2)}) async-start(), calls=%async_computation.7 | async-start | bytes 4325376 | tf_op jit(solution)/shard_map/all_gather | solution.py:109
  12.8 884.6 %all-reduce.3.cloned.1.call-start = ((), (), s32[]{:S(2)}) async-start(), calls=%async_computation.14 | async-start | bytes 3670016
  132.2 1.9 copy-start
  134.1 34.5 %collective-permute-start = (bf16[2,128,2,512]{3,1,2,0:T(8,128)(2,1)S(1)}, bf16[2,128,2,512]{3,1,2,0:T(8,128)(2,1)S(1)}, u32[]{:S(2)}, u32[]{:S(2)}) collective-permute-start(bf16[2,128,2,512]{3,1,2,0:T(8,128)(2,1)S(1)} %slice.50), channel_id=1, source_target_pairs={{0,4},{4,8},{8,12},{12,16},{16,20},{20,24},{24,28},{28,32},{32,36}... | collective-permute-start | bytes 1572872 | tf_op jit(solution)/shard_map/ppermute | solution.py:21
  408.9 2.6 copy-start.5
  412.4 1.4 copy-start.4
  415.4 1.6 copy-start.3
  475.5 41.2 %collective-permute-start.1 = (bf16[2,128,2,512]{1,0,3,2:T(2,128)(2,1)}, bf16[2,128,2,512]{1,0,3,2:T(2,128)(2,1)S(1)}, u32[]{:S(2)}, u32[]{:S(2)}) collective-permute-start(bf16[2,128,2,512]{1,0,3,2:T(2,128)(2,1)} %convert_element_type.110), channel_id=1, source_target_pairs={{4,0},{8,4},{12,8},{16,12},{20,16},{24,20},{28,24},{32,28},{36,32}... | collective-permute-start | bytes 1572872 | tf_op jit(solution)/shard_map/ppermute | solution.py:21
  517.0 8.8 copy-start.14
  523.9 2.0 copy-start.8
  537.3 408.5 %reduce-scatter.7.cloned.1.call-start = ((), (), s32[]{:S(2)}) async-start(), calls=%async_computation.11 | async-start | bytes 5242880 | tf_op jit(solution)/shard_map/reduce_scatter | solution.py:185
  575.9 446.8 %reduce-scatter.5.cloned.1.call-start = ((), (), s32[]{:S(2)}) async-start(), calls=%async_computation.9 | async-start | bytes 5242880 | tf_op jit(solution)/shard_map/reduce_scatter | solution.py:143
  597.4 617.5 %reduce-scatter.11.cloned.1.call-start = ((), (), s32[]{:S(2)}) async-start(), calls=%async_computation.13 | async-start | bytes 8650752 | tf_op jit(solution)/shard_map/reduce_scatter | solution.py:205
  597.6 4.7 copy-start.13
  612.9 1.5 copy-start.15
  612.9 643.4 %reduce-scatter.9.cloned.1.call-start = ((), (), s32[]{:S(2)}) async-start(), calls=%async_computation.12 | async-start | bytes 4587520 | tf_op jit(solution)/shard_map/reduce_scatter | solution.py:222
  623.2 0.7 copy-start.16
  623.2 322.6 %copy-start.2 = (bf16[128,4096]{1,0:T(8,128)(2,1)S(1)}, bf16[128,4096]{1,0:T(8,128)(2,1)}, u32[]{:S(2)}) copy-start(bf16[128,4096]{1,0:T(8,128)(2,1)} %param.7) | copy-start | bytes 3145732
  623.2 322.6 %copy-start.10 = (f32[4096]{0:T(1024)S(1)}, f32[4096]{0:T(1024)}, u32[]{:S(2)}) copy-start(f32[4096]{0:T(1024)} %param.8) | copy-start | bytes 49156
  623.2 322.6 %copy-start.12 = (f32[128]{0:T(128)S(1)}, f32[128]{0:T(128)}, u32[]{:S(2)}) copy-start(f32[128]{0:T(128)} %copy-done.11) | copy-start | bytes 1540
  623.2 399.5 %copy-start.6 = (bf16[128,4096]{1,0:T(8,128)(2,1)S(1)}, bf16[128,4096]{1,0:T(8,128)(2,1)}, u32[]{:S(2)}) copy-start(bf16[128,4096]{1,0:T(8,128)(2,1)} %param.13) | copy-start | bytes 3145732
  945.7 77.0 %copy-start.7 = (bf16[128,4096]{1,0:T(8,128)(2,1)S(1)}, bf16[128,4096]{1,0:T(8,128)(2,1)}, u32[]{:S(2)}) copy-start(bf16[128,4096]{1,0:T(8,128)(2,1)} %reduce-scatter.7.cloned.1.call-done) | copy-start | bytes 3145732
Sparse Core Ops, SparseCore 0:
  11.2 72.4 all-gather.8
  85.4 39.6 all-gather.6
  126.7 58.4 all-gather.16
  188.1 81.1 all-gather.14
  271.4 44.7 all-gather.10
  319.2 81.8 all-gather.12
  537.4 359.9 all-reduce.2
  899.9 45.7 reduce-scatter.6
  948.1 46.9 reduce-scatter.4
  997.6 217.2 reduce-scatter.10
  1218.0 38.2 reduce-scatter.8
where the time goes:
time: 1270 us; the launch traced here: 1260 us
  waiting for transfers between devices  856 us (67%)
  matrix products  160 us (13%)
  local copies, waits for them, and re-layouts  117 us (9%)
  blocking collectives  74.8 us (6%)
  other arithmetic  34 us (3%)
  between operations  15 us (1%)
    unnamed x12, waiting for transfers between devices  276 us
    reduce_scatter x1, waiting for transfers between devices, per_device(): lax.psum_scatter(jnp.stack([query_part, output_part], axis=1).astype(jnp....  189 us
    all_gather x1, waiting for transfers between devices, per_device(): lax.all_gather(query_weight, 'seq', axis=0, tiled=True)  84.9 us
    psum x1, blocking collectives, per_device(): gain_grad = lax.psum(jnp.sum(feature_grad * scaled, axis=0), ('seq', 'tp'))  74.8 us
    all_gather x1, waiting for transfers between devices, per_device(): lax.all_gather(keyval_weight, 'seq', axis=0, tiled=True)  70.9 us
    all_gather x1, waiting for transfers between devices, per_device(): lax.all_gather(output_weight, 'seq', axis=0, tiled=True)  67.2 us
    reduce_scatter x1, waiting for transfers between devices, per_device(): lax.psum_scatter(jnp.einsum('th,dh->td', rows_part, full_query, preferred...  46.8 us
    all_gather x1, waiting for transfers between devices, per_device(): lax.all_gather(neighbours, 'tp', axis=0, tiled=True)  41.3 us
  transfers between devices with their start and end apart: 13, of which 9 were waited for; matrix products, arithmetic and copies ran while one was open for 17% of the time, Pallas kernels for 0%

commit v1 on v0

v1 whole, which is shorter than its diff:
```python
import functools
import math

import jax
import jax.numpy as jnp
from jax import lax
from jax.experimental import pallas as pl
from jax.experimental.pallas import tpu as pltpu
from jax.sharding import PartitionSpec as P

HEAD_DIM = 128
SPAN = 64
K_NB = 2
R = 128
LENGTH = 2048
EPSILON = 1e-06
LANES = 128

Z_NEAR, Z_WRAP = 8, 24
Y_NEAR, Y_WRAP = 2, 6
X_HIGH = 1
X_LOW, CORE = 2, 1


def seq_swap(value, mask):
    count = lax.axis_size("seq")
    return lax.ppermute(value, "seq", [(i, i ^ mask) for i in range(count)])


def tp_swap(value, mask):
    count = lax.axis_size("tp")
    return lax.ppermute(value, "tp", [(i, i ^ mask) for i in range(count)])


def f32_sum(*terms):
    total = terms[0].astype(jnp.float32)
    for term in terms[1:]:
        total = total + term.astype(jnp.float32)
    return total


def ring_gather(block, near, wrap):
    half = block.shape[0] // 2
    from_near, from_wrap = seq_swap(block, near), seq_swap(block, wrap)
    low, high = seq_swap(from_wrap[:half], near), seq_swap(from_near[half:], wrap)
    return jnp.concatenate([block, from_near, low, high, from_wrap], axis=0)


def ring_scatter(parts, near, wrap):
    rows = parts.shape[0] // 4
    half = rows // 2
    own, to_near, far, to_wrap = [parts[i * rows : (i + 1) * rows] for i in range(4)]
    low, high = seq_swap(far[:half], wrap), seq_swap(far[half:], near)
    to_near = jnp.concatenate(
        [f32_sum(to_near[:half], low).astype(jnp.bfloat16), to_near[half:]], axis=0
    )
    to_wrap = jnp.concatenate(
        [to_wrap[:half], f32_sum(to_wrap[half:], high).astype(jnp.bfloat16)], axis=0
    )
    return f32_sum(own, seq_swap(to_near, near), seq_swap(to_wrap, wrap)).astype(jnp.bfloat16)


def gather_seq(shard, y_outer):
    block = jnp.concatenate([shard, seq_swap(shard, X_HIGH)], axis=0)
    if y_outer:
        return ring_gather(ring_gather(block, Z_NEAR, Z_WRAP), Y_NEAR, Y_WRAP)
    return ring_gather(ring_gather(block, Y_NEAR, Y_WRAP), Z_NEAR, Z_WRAP)


def scatter_seq(parts, y_outer):
    if y_outer:
        parts = ring_scatter(ring_scatter(parts, Y_NEAR, Y_WRAP), Z_NEAR, Z_WRAP)
    else:
        parts = ring_scatter(ring_scatter(parts, Z_NEAR, Z_WRAP), Y_NEAR, Y_WRAP)
    rows = parts.shape[0] // 2
    return f32_sum(parts[:rows], seq_swap(parts[rows:], X_HIGH))


def gather_tp(shard):
    across = tp_swap(shard, X_LOW)
    return jnp.concatenate([shard, across, tp_swap(shard, CORE), tp_swap(across, CORE)], axis=0)


def scatter_tp(parts):
    half = parts.shape[0] // 2
    quarter = half // 2
    beside = tp_swap(parts[half:], CORE)
    sent = f32_sum(parts[quarter:half], beside[quarter:]).astype(jnp.bfloat16)
    kept = f32_sum(parts[:quarter], beside[:quarter]).astype(jnp.bfloat16)
    return kept, tp_swap(sent, X_LOW)


def mask_of(place, y_outer):
    if not y_outer:
        return place
    y, z, x = place // 8, (place // 2) % 4, place % 2
    return z * 8 + y * 2 + x


def norm_kernel(seq_ref, residual_ref, gain_ref, cotangent_ref, normed_ref, turned_ref):
    me = seq_ref[0]
    width = residual_ref.shape[1]
    total = jnp.zeros((residual_ref.shape[0], LANES), jnp.float32)
    for place in range(width // LANES):
        piece = residual_ref[:, place * LANES : (place + 1) * LANES].astype(jnp.float32)
        total = total + piece * piece
    inverse_rms = lax.rsqrt(jnp.sum(total, axis=-1, keepdims=True) / width + EPSILON)
    for place in range(width // LANES):
        here = slice(place * LANES, (place + 1) * LANES)
        there = pl.ds(pl.multiple_of((me ^ mask_of(place, True)) * LANES, LANES), LANES)
        scaled = residual_ref[:, there].astype(jnp.float32) * inverse_rms
        normed_ref[:, here] = (scaled * gain_ref[:, there]).astype(jnp.bfloat16)
        there = pl.ds(pl.multiple_of((me ^ mask_of(place, False)) * LANES, LANES), LANES)
        turned_ref[:, here] = cotangent_ref[:, there]


def output_kernel(seq_ref, residual_ref, kept_ref, across_ref, out_ref):
    me = seq_ref[0]
    for place in range(residual_ref.shape[1] // LANES):
        here = slice(place * LANES, (place + 1) * LANES)
        there = pl.ds(pl.multiple_of((me ^ mask_of(place, False)) * LANES, LANES), LANES)
        mixed = kept_ref[:, here].astype(jnp.float32) + across_ref[:, here].astype(jnp.float32)
        out_ref[:, there] = (residual_ref[:, there].astype(jnp.float32) + mixed).astype(
            jnp.bfloat16
        )


def residual_kernel(
    seq_ref, residual_ref, gain_ref, cotangent_ref, kept_ref, across_ref, out_ref, gained_ref
):
    me = seq_ref[0]
    width = residual_ref.shape[1]
    rows = residual_ref.shape[0]
    square = jnp.zeros((rows, LANES), jnp.float32)
    cross = jnp.zeros((rows, LANES), jnp.float32)
    for place in range(width // LANES):
        here = slice(place * LANES, (place + 1) * LANES)
        there = pl.ds(pl.multiple_of((me ^ mask_of(place, True)) * LANES, LANES), LANES)
        feature = kept_ref[:, here].astype(jnp.float32) + across_ref[:, here].astype(jnp.float32)
        gained = feature * gain_ref[:, there]
        piece = residual_ref[:, there].astype(jnp.float32)
        square = square + piece * piece
        cross = cross + gained * piece
        gained_ref[:, there] = gained
    inverse_rms = lax.rsqrt(jnp.sum(square, axis=-1, keepdims=True) / width + EPSILON)
    mean = jnp.sum(cross, axis=-1, keepdims=True) * inverse_rms / width
    for place in range(width // LANES):
        here = slice(place * LANES, (place + 1) * LANES)
        scaled = residual_ref[:, here].astype(jnp.float32) * inverse_rms
        out_ref[:, here] = (
            inverse_rms * (gained_ref[:, here] - scaled * mean)
            + cotangent_ref[:, here].astype(jnp.float32)
        ).astype(jnp.bfloat16)


def whole(shape):
    return pl.BlockSpec(shape, lambda *_: (0,) * len(shape))


def row_call(kernel, seq_index, args, outs, scratch=()):
    return pl.pallas_call(
        kernel,
        grid_spec=pltpu.PrefetchScalarGridSpec(
            num_scalar_prefetch=1,
            grid=(1,),
            in_specs=[whole(arg.shape) for arg in args],
            out_specs=[whole(out.shape) for out in outs],
            scratch_shapes=list(scratch),
        ),
        out_shape=outs,
        compiler_params=pltpu.CompilerParams(vmem_limit_bytes=40 * 1024 * 1024),
    )(seq_index, *args)


def dot(left, right, left_dim, right_dim):
    return lax.dot_general(
        left, right, (((left_dim,), (right_dim,)), ((), ())), preferred_element_type=jnp.float32
    )


def attention_kernel(
    place_ref,
    query_ref,
    query_next_ref,
    up_ref,
    up_next_ref,
    keyval_ref,
    attended_ref,
    query_back_ref,
    keyval_back_ref,
    attended_end_ref,
    query_back_end_ref,
    attended_carry,
    query_carry,
):
    span = pl.program_id(0)
    last = pl.num_programs(0) - 1
    width = query_ref.shape[1]
    rows = lax.broadcasted_iota(jnp.int32, (SPAN, width), 0)
    here = pl.ds(pl.multiple_of(place_ref[span] * SPAN, SPAN), SPAN)
    after = pl.ds(pl.multiple_of(place_ref[span + 1] * SPAN, SPAN), SPAN)

    @pl.when(span == 0)
    def _():
        attended_carry[...] = jnp.zeros_like(attended_carry)
        query_carry[...] = jnp.zeros_like(query_carry)

    def shifted(ref, next_ref):
        first = ref[here, :].astype(jnp.float32)
        second = jnp.where(span == last, next_ref[...], ref[after, :]).astype(jnp.float32)
        joined = jnp.where(rows == SPAN - 1, first, second)
        return pltpu.roll(joined, 1, 0).astype(jnp.bfloat16)

    query = shifted(query_ref, query_next_ref)
    up = shifted(up_ref, up_next_ref)
    factor = 1.0 / math.sqrt(HEAD_DIM)
    attended_parts, query_parts = [], []
    for head in range(width // HEAD_DIM):
        own = slice(head * HEAD_DIM, (head + 1) * HEAD_DIM)
        value_own = slice(width + head * HEAD_DIM, width + (head + 1) * HEAD_DIM)
        q, u = query[:, own], up[:, own]
        keys, values = keyval_ref[:, own], keyval_ref[:, value_own]
        scores = dot(q, keys, 1, 1) * factor
        exponent = jnp.exp(scores - jnp.max(scores, axis=-1, keepdims=True))
        probabilities = exponent / jnp.sum(exponent, axis=-1, keepdims=True)
        weights = probabilities.astype(jnp.bfloat16)
        attended_parts.append(dot(weights, values, 1, 0))
        weight_grad = dot(u, values, 1, 1)
        inner = jnp.sum(weight_grad * probabilities, axis=-1, keepdims=True)
        score_grad = (probabilities * (weight_grad - inner) * factor).astype(jnp.bfloat16)
        query_parts.append(dot(score_grad, keys, 1, 0))
        keyval_back_ref[:, own] = dot(score_grad, q, 0, 0).astype(jnp.bfloat16)
        keyval_back_ref[:, value_own] = dot(weights, u, 0, 0).astype(jnp.bfloat16)
    for parts, carry, out_ref, end_ref in (
        (attended_parts, attended_carry, attended_ref, attended_end_ref),
        (query_parts, query_carry, query_back_ref, query_back_end_ref),
    ):
        turned = pltpu.roll(jnp.concatenate(parts, axis=1), SPAN - 1, 0)
        out_ref[...] = jnp.where(rows == SPAN - 1, turned, carry[...]).astype(jnp.bfloat16)
        carry[...] = turned
        end_ref[...] = jnp.where(rows == SPAN - 1, 0.0, turned).astype(jnp.bfloat16)


def attention(places, query, query_next, up, up_next, keyvals):
    tokens, width = query.shape
    spans = tokens // SPAN
    span_rows = keyvals.shape[0] // spans
    by_place = lambda i, places: (places[i], 0)
    like = lambda array: jax.ShapeDtypeStruct(array.shape, jnp.bfloat16)
    return pl.pallas_call(
        attention_kernel,
        grid_spec=pltpu.PrefetchScalarGridSpec(
            num_scalar_prefetch=1,
            grid=(spans,),
            in_specs=[
                whole(query.shape),
                whole(query_next.shape),
                whole(up.shape),
                whole(up_next.shape),
                pl.BlockSpec((span_rows, keyvals.shape[1]), by_place),
            ],
            out_specs=[
                pl.BlockSpec((SPAN, width), by_place),
                pl.BlockSpec((SPAN, width), by_place),
                pl.BlockSpec((span_rows, keyvals.shape[1]), by_place),
                whole(query_next.shape),
                whole(query_next.shape),
            ],
            scratch_shapes=[
                pltpu.VMEM((SPAN, width), jnp.float32),
                pltpu.VMEM((SPAN, width), jnp.float32),
            ],
        ),
        out_shape=[
            like(query),
            like(query),
            like(keyvals),
            like(query_next),
            like(query_next),
        ],
        compiler_params=pltpu.CompilerParams(vmem_limit_bytes=40 * 1024 * 1024),
    )(places, query, query_next, up, up_next, keyvals)


def per_device(
    residual, norm_gain, query_weight, keyval_weight, output_weight, neighbours, cotangent
):
    me, seq_count = lax.axis_index("seq"), lax.axis_size("seq")
    column, tp_count = lax.axis_index("tp"), lax.axis_size("tp")
    tokens_here, features = residual.shape
    local_width = query_weight.shape[1]
    neighbour_count, _, enc_width = neighbours.shape
    enc_rows = keyval_weight.shape[0]
    group_tokens = tokens_here * tp_count
    spans = group_tokens // SPAN
    seq_index = me.astype(jnp.int32).reshape(1)
    gain_row = norm_gain.reshape(1, features)
    token_shape = jax.ShapeDtypeStruct(residual.shape, jnp.bfloat16)

    flat_neighbours = neighbours.reshape(neighbour_count * R, enc_width)
    group_neighbours = gather_tp(flat_neighbours)
    full_keyval = lax.all_gather(
        keyval_weight.reshape(enc_rows, 2 * local_width), "seq", axis=0, tiled=False
    ).reshape(seq_count * enc_rows, 2 * local_width)
    normed, turned = row_call(
        norm_kernel, seq_index, (residual, gain_row, cotangent), [token_shape, token_shape]
    )
    group_normed = gather_tp(normed)
    group_cotangent = gather_tp(turned)
    full_query = gather_seq(query_weight, True)
    full_output = gather_seq(output_weight, False)

    keyvals = dot(group_neighbours, full_keyval, 1, 0).astype(jnp.bfloat16)
    query = dot(group_normed, full_query, 1, 0).astype(jnp.bfloat16)
    attended_grad = dot(group_cotangent, full_output, 1, 0).astype(jnp.bfloat16)

    block = jnp.arange(spans, dtype=jnp.int32)
    mask = (block // (spans // tp_count)) ^ column.astype(jnp.int32)
    place = ((mask % 2) * 2 + mask // 2) * (spans // tp_count) + block % (spans // tp_count)
    places = jnp.concatenate([place, place[:1]])
    groups = LENGTH // group_tokens
    inside = [i for i in range(seq_count) if i % groups]
    first_row = place[0] * SPAN

    def first_block(value):
        return lax.dynamic_slice(value, (first_row, 0), (SPAN, local_width))

    def from_next(value):
        return lax.ppermute(first_block(value), "seq", [(i, i - 1) for i in inside])

    attended, query_back, keyval_back, attended_end, query_back_end = attention(
        places, query, from_next(query), attended_grad, from_next(attended_grad), keyvals
    )

    def with_previous(value, end):
        arrived = lax.ppermute(end, "seq", [(i - 1, i) for i in inside])
        return lax.dynamic_update_slice(value, first_block(value) + arrived, (first_row, 0))

    attended = with_previous(attended, attended_end)
    query_back = with_previous(query_back, query_back_end)

    keyval_part = dot(group_neighbours, keyval_back, 0, 0).astype(jnp.bfloat16)
    keyval_grad = lax.psum_scatter(
        keyval_part.reshape(seq_count, enc_rows, 2 * local_width),
        "seq",
        scatter_dimension=0,
        tiled=False,
    )
    neighbour_kept, neighbour_across = scatter_tp(
        dot(keyval_back, full_keyval, 1, 1).astype(jnp.bfloat16)
    )
    output_part = dot(group_cotangent, attended, 0, 0).astype(jnp.bfloat16)
    query_part = dot(group_normed, query_back, 0, 0).astype(jnp.bfloat16)
    output_grad = scatter_seq(output_part, False)
    query_grad = scatter_seq(query_part, True)
    mixed_kept, mixed_across = scatter_tp(dot(attended, full_output, 1, 1).astype(jnp.bfloat16))
    feature_kept, feature_across = scatter_tp(
        dot(query_back, full_query, 1, 1).astype(jnp.bfloat16)
    )

    row_sums = jnp.sum(f32_sum(full_query) * f32_sum(query_part), axis=1)
    where_from = mask_of(jnp.arange(seq_count, dtype=jnp.int32) ^ me, True)
    gain_part = jnp.take(row_sums.reshape(seq_count, features // seq_count), where_from, axis=0)
    gain_grad = lax.psum(gain_part.reshape(features), ("seq", "tp")) / norm_gain

    (layer_output,) = row_call(
        output_kernel, seq_index, (residual, mixed_kept, mixed_across), [token_shape]
    )
    (residual_grad,) = row_call(
        residual_kernel,
        seq_index,
        (residual, gain_row, cotangent, feature_kept, feature_across),
        [token_shape],
        [pltpu.VMEM(residual.shape, jnp.float32)],
    )
    neighbour_grad = (
        f32_sum(neighbour_kept, neighbour_across).astype(jnp.bfloat16).reshape(neighbours.shape)
    )
    return (
        layer_output,
        residual_grad,
        neighbour_grad,
        gain_grad,
        query_grad,
        keyval_grad.astype(jnp.float32).reshape(enc_rows, 2, local_width),
        output_grad,
    )


def solution(mesh):
    in_specs = (
        P(("seq", "tp"), None),
        P(),
        P("seq", "tp"),
        P("seq", None, "tp"),
        P("seq", "tp"),
        P(("seq", "tp"), None, None),
        P(("seq", "tp"), None),
    )
    out_specs = (
        P(("seq", "tp"), None),
        P(("seq", "tp"), None),
        P(("seq", "tp"), None, None),
        P(),
        P("seq", "tp"),
        P("seq", None, "tp"),
        P("seq", "tp"),
    )
    return jax.shard_map(
        per_device, mesh=mesh, in_specs=in_specs, out_specs=out_specs, check_vma=False
    )
```

time: 1270 us -> 458 us (0.36)
  waiting for transfers between devices: 856 us -> 168 us
  matrix products: 160 us -> 38.7 us
  local copies, waits for them, and re-layouts: 117 us -> 44.7 us
  starting transfers between devices: 6.91 us -> 71.7 us
  Pallas kernels: 0 us -> 23.1 us
  other arithmetic: 34 us -> 14 us
    all_gather x6 -> x1, waiting for transfers between devices: 305 us -> 0.02 us  [per_device(): lax.all_gather(keyval_weight.reshape(enc_rows, 2 * local_width), 'seq', a...]
    unnamed x12 -> x2, waiting for transfers between devices: 276 us -> 0.03 us
    reduce_scatter x4 -> x1, waiting for transfers between devices: 275 us -> 0.01 us  [per_device(): lax.psum_scatter(keyval_part.reshape(seq_count, enc_rows, 2 * local_width...]
    ppermute x2 -> x55, waiting for transfers between devices: 0.01 us -> 168 us  [the longest x36 155 us: seq_swap(): return lax.ppermute(value, 'seq', [(i, i ^ mask) for i in range(count)])]
    dot_general x21 -> x9, matrix products: 160 us -> 38.7 us  [dot(): lax.dot_general(left, right, (((left_dim,), (right_dim,)), ((), ())), pre...]
    ppermute x2 -> x55, starting transfers between devices: 5.9 us -> 71.7 us  [the longest x36 50.8 us: seq_swap(): return lax.ppermute(value, 'seq', [(i, i ^ mask) for i in range(count)])]
    pallas_call x0 -> x4, Pallas kernels: none -> 23.1 us  [the longest x1 18 us: attention(): pl.pallas_call(attention_kernel, grid_spec=pltpu.PrefetchScalarGridSpec(n...]
    slice x6 -> x17, local copies, waits for them, and re-layouts: 29.5 us -> 8.36 us  [the longest x3 3.13 us: scatter_tp(): beside = tp_swap(parts[half:], CORE)]
  transfers between devices with their start and end apart: 13 -> 57, of which waited for: 9 -> 21; matrix products, arithmetic and copies ran while one was open for 17% -> 19% of each run, Pallas kernels for 0% -> 1%
where the time goes in v1:
time: 458 us; the launch traced here: 448 us
  waiting for transfers between devices  168 us (37%)
  blocking collectives  72.9 us (16%)
  starting transfers between devices  71.7 us (16%)
  local copies, waits for them, and re-layouts  44.7 us (10%)
  matrix products  38.7 us (8%)
  Pallas kernels  23.1 us (5%)
  between operations  15.5 us (3%)
  other arithmetic  14 us (3%)
    ppermute x36, waiting for transfers between devices, seq_swap(): return lax.ppermute(value, 'seq', [(i, i ^ mask) for i in range(count)])  155 us
    psum x1, blocking collectives, per_device(): gain_grad = lax.psum(gain_part.reshape(features), ('seq', 'tp')) / norm_gain  72.9 us
    ppermute x36, starting transfers between devices, seq_swap(): return lax.ppermute(value, 'seq', [(i, i ^ mask) for i in range(count)])  50.8 us
    dot_general x9, matrix products, dot(): lax.dot_general(left, right, (((left_dim,), (right_dim,)), ((), ())), pre...  38.7 us
    unnamed x79, local copies, waits for them, and re-layouts  24.4 us
    pallas_call x1, Pallas kernels, attention(): pl.pallas_call(attention_kernel, grid_spec=pltpu.PrefetchScalarGridSpec(n...  18 us
    ppermute x15, waiting for transfers between devices, tp_swap(): return lax.ppermute(value, 'tp', [(i, i ^ mask) for i in range(count)])  12.8 us
    ppermute x2, starting transfers between devices, with_previous(): arrived = lax.ppermute(end, 'seq', [(i - 1, i) for i in inside])  12.1 us
  transfers between devices with their start and end apart: 57, of which 21 were waited for; matrix products, arithmetic and copies ran while one was open for 19% of the time, Pallas kernels for 1%

profile of v1, /device:TPU:0, one launch (start us, length us, event | category | flops | bytes accessed | tf_op | source)
XLA Modules:
  0.0 448.4 jit_solution(15558462578773292533)
XLA Ops:
  12.9 2.7 collective-permute-start.16
  18.0 1.7 constant_dynamic-update-slice_fusion.33
  22.5 20.4 %collective-permute-done.16 = bf16[128,512]{1,0:T(8,128)(2,1)S(1)} collective-permute-done((bf16[128,512]{1,0:T(8,128)(2,1)}, bf16[128,512]{1,0:T(8,128)(2,1)S(1)}, u32[]{:S(2)}, u32[]{:S(2)}) %collective-permute-start.16) | collective-permute-done | bytes 131104 | tf_op jit(solution)/shard_map/ppermute | solution.py:27
  43.7 3.0 collective-permute-start.18
  49.1 1.9 collective-permute-start.4
  51.5 4.0 collective-permute-start.5
  56.2 2.0 constant_dynamic-update-slice_fusion.31
  59.1 3.1 collective-permute-start.20
  62.3 1.9 constant_dynamic-update-slice_fusion.9
  67.7 3.5 collective-permute-done.6
  73.7 5.8 %collective-permute-done.7 = bf16[128,512]{1,0:T(8,128)(2,1)S(1)} collective-permute-done((bf16[128,512]{1,0:T(8,128)(2,1)S(1)}, bf16[128,512]{1,0:T(8,128)(2,1)S(1)}, u32[]{:S(2)}, u32[]{:S(2)}) %collective-permute-start.7) | collective-permute-done | bytes 131104 | tf_op jit(solution)/shard_map/ppermute | solution.py:27
  80.2 1.8 constant_dynamic-update-slice_fusion.6
  82.4 2.8 collective-permute-start.9
  86.8 9.1 %collective-permute-done = bf16[128,4096]{1,0:T(8,128)(2,1)S(1)} collective-permute-done((bf16[128,4096]{1,0:T(8,128)(2,1)S(1)}, bf16[128,4096]{1,0:T(8,128)(2,1)S(1)}, u32[]{:S(2)}, u32[]{:S(2)}) %collective-permute-start) | collective-permute-done | bytes 1048608 | tf_op jit(solution)/shard_map/ppermute | solution.py:32
  95.8 8.5 %collective-permute-done.22 = bf16[1024,512]{1,0:T(8,128)(2,1)S(1)} collective-permute-done((bf16[1024,512]{1,0:T(8,128)(2,1)}, bf16[1024,512]{1,0:T(8,128)(2,1)S(1)}, u32[]{:S(2)}, u32[]{:S(2)}) %collective-permute-start.22) | collective-permute-done | bytes 1048608 | tf_op jit(solution)/shard_map/ppermute | solution.py:27
  109.4 3.7 collective-permute-done.26
  113.0 11.0 %collective-permute-done.8 = bf16[1024,512]{1,0:T(8,128)(2,1)S(1)} collective-permute-done((bf16[1024,512]{1,0:T(8,128)(2,1)S(1)}, bf16[1024,512]{1,0:T(8,128)(2,1)S(1)}, u32[]{:S(2)}, u32[]{:S(2)}) %collective-permute-start.8) | collective-permute-done | bytes 1048608 | tf_op jit(solution)/shard_map/ppermute | solution.py:27
  126.6 2.7 collective-permute-start.11
  129.5 2.3 convolution_convert_fusion.7.up_ref
  131.8 7.0 %collective-permute-done.10 = bf16[512,512]{1,0:T(8,128)(2,1)S(1)} collective-permute-done((bf16[512,512]{1,0:T(8,128)(2,1)S(1)}, bf16[512,512]{1,0:T(8,128)(2,1)S(1)}, u32[]{:S(2)}, u32[]{:S(2)}) %collective-permute-start.10) | collective-permute-done | bytes 524320 | tf_op jit(solution)/shard_map/ppermute | solution.py:27
  138.8 1.7 collective-permute-start.25
  141.7 2.3 convolution_convert_fusion.8.query_ref
  146.2 3.7 reshape.209
  149.9 6.9 %convolution_convert_fusion.4.keyval_ref = bf16[2048,1024]{1,0:T(8,128)(2,1)S(1)} fusion(bf16[896,1024]{1,0:T(8,128)(2,1)} %reshape.209, bf16[512,896]{1,0:T(8,128)(2,1)} %collective-permute-done.28, bf16[512,896]{1,0:T(8,128)(2,1)} %collective-permute-done.27, bf16[512,896]{1,0:T(8,128)(2,1)} %collective-permute-done.26, bf16[512,896]{1,0:T(8,128)(2,1)S(1)} %bitcast.33), kind=kOutput, calls=%fused_computation.6 | convolution fusion | flops 3774873600 | bytes 9699328 | tf_op jit(solution)/shard_map/dot_general | solution.py:176
  156.9 18.0 %shard_map.127 = (bf16[512,512]{1,0:T(8,128)(2,1)S(1)}, bf16[512,512]{1,0:T(8,128)(2,1)S(1)}, bf16[2048,1024]{1,0:T(8,128)(2,1)S(1)}, bf16[64,512]{1,0:T(8,128)(2,1)S(1)}, bf16[64,512]{1,0:T(8,128)(2,1)S(1)}) custom-call(s32[9]{0:T(128)S(1)} %pad_add_fusion.place_ref, bf16[512,512]{1,0:T(8,128)(2,1)S(1)} %convolution_convert_fusion.8.query_ref, ...), custom_call_target="tpu_custom_call" | custom-call | tf_op jit(solution)/shard_map/pallas_call | solution.py:250
  174.9 6.1 %collective-permute-start.29 = (bf16[64,512]{1,0:T(8,128)(2,1)S(1)}, bf16[64,512]{1,0:T(8,128)(2,1)S(1)}, u32[]{:S(2)}, u32[]{:S(2)}) collective-permute-start(bf16[64,512]{1,0:T(8,128)(2,1)S(1)} %get-tuple-element.17), channel_id=1, source_target_pairs={{0,4},{4,8},{8,12},{16,20},{20,24},{24,28},{32,36},{36,40},{40,44}... | collective-permute-start | bytes 196616 | tf_op jit(solution)/shard_map/ppermute | solution.py:336
  181.0 6.1 %collective-permute-start.32 = (bf16[64,512]{1,0:T(8,128)(2,1)S(1)}, bf16[64,512]{1,0:T(8,128)(2,1)S(1)}, u32[]{:S(2)}, u32[]{:S(2)}) collective-permute-start(bf16[64,512]{1,0:T(8,128)(2,1)S(1)} %get-tuple-element.19), channel_id=1, source_target_pairs={{0,4},{4,8},{8,12},{16,20},{20,24},{24,28},{32,36},{36,40},{40,44}... | collective-permute-start | bytes 196616 | tf_op jit(solution)/shard_map/ppermute | solution.py:336
  187.1 4.8 %convolution_convert_fusion.5 = bf16[2048,896]{1,0:T(8,128)(2,1)S(1)} fusion(bf16[2048,1024]{1,0:T(8,128)(2,1)S(1)} %get-tuple-element.20, bf16[896,1024]{1,0:T(8,128)(2,1)S(1)} %copy-done.13), kind=kOutput, calls=%fused_computation.8 | convolution fusion | flops 3759931392 | bytes 9699328 | tf_op jit(solution)/shard_map/dot_general | solution.py:176
  191.9 1.8 copy-done.10
  195.2 5.7 %convolution_convert_fusion.6 = bf16[896,1024]{1,0:T(8,128)(2,1)S(1)} fusion(bf16[2048,1024]{1,0:T(8,128)(2,1)S(1)} %get-tuple-element.20, bf16[512,896]{1,0:T(8,128)(2,1)} %collective-permute-done.28, bf16[512,896]{1,0:T(8,128)(2,1)} %collective-permute-done.27, bf16[512,896]{1,0:T(8,128)(2,1)} %collective-permute-done.26, bf16[512,896]{1,0:T(8,128)(2,1)S(1)} %bitcast.34), kind=kOutput, calls=%fused_computation.18 | convolution fusion | flops 3773693952 | bytes 9699328 | tf_op jit(solution)/shard_map/dot_general | solution.py:176
  202.6 4.7 %convolution_convert_fusion = bf16[4096,512]{1,0:T(8,128)(2,1)S(1)} fusion(bf16[512,4096]{1,0:T(8,128)(2,1)} %copy-done.18, bf16[512,512]{1,0:T(8,128)(2,1)S(1)} %add_dynamic-update-slice_fusion.1), kind=kOutput, calls=%fused_computation.2 | convolution fusion | flops 2149580800 | bytes 8912896 | tf_op jit(solution)/shard_map/dot_general | solution.py:176
  208.5 2.3 collective-permute-start.46
  211.9 2.8 multiply_reduce_fusion
  214.7 2.0 copy-done.8
  217.8 1.7 collective-permute-start.37
  221.9 72.9 %psum.7 = f32[4096]{0:T(1024)S(1)} all-reduce(f32[4096]{0:T(1024)S(1)} %select_bitcast_fusion), channel_id=1, replica_groups=mesh['seq'=32,'tp'=4] {'seq','tp'}, use_global_device_ids=true, to_apply=%region_1.2 | all-reduce | flops 4096 | bytes 32768 | tf_op jit(solution)/shard_map/psum | solution.py:364
  295.4 4.6 %convolution_convert_fusion.2 = bf16[512,4096]{1,0:T(8,128)(2,1)S(1)} fusion(bf16[512,512]{1,0:T(8,128)(2,1)S(1)} %add_dynamic-update-slice_fusion, bf16[4096,512]{1,0:T(8,128)(2,1)} %copy-done.22), kind=kOutput, calls=%fused_computation.4 | convolution fusion | flops 2149580800 | bytes 8912896 | tf_op jit(solution)/shard_map/dot_general | solution.py:176
  302.9 1.9 add_convert_fusion.10
  311.7 4.6 %convolution_convert_fusion.3 = bf16[512,4096]{1,0:T(8,128)(2,1)S(1)} fusion(bf16[512,512]{1,0:T(8,128)(2,1)S(1)} %add_dynamic-update-slice_fusion.1, bf16[4096,512]{1,0:T(8,128)(2,1)} %copy-done.25), kind=kOutput, calls=%fused_computation.5 | convolution fusion | flops 2149580800 | bytes 8912896 | tf_op jit(solution)/shard_map/dot_general | solution.py:176
  316.5 15.0 %collective-permute-done.47 = bf16[1024,512]{1,0:T(8,128)(2,1)S(1)} collective-permute-done((bf16[1024,512]{1,0:T(8,128)(2,1)S(1)}, bf16[1024,512]{1,0:T(8,128)(2,1)S(1)}, u32[]{:S(2)}, u32[]{:S(2)}) %collective-permute-start.47) | collective-permute-done | bytes 1048608 | tf_op jit(solution)/shard_map/ppermute | solution.py:27
  331.4 3.9 collective-permute-done.49
  335.9 2.6 collective-permute-start.50
  339.4 3.6 collective-permute-done.50
  345.6 4.7 %collective-permute-done.41 = bf16[128,512]{1,0:T(8,128)(2,1)S(1)} collective-permute-done((bf16[128,512]{1,0:T(8,128)(2,1)S(1)}, bf16[128,512]{1,0:T(8,128)(2,1)S(1)}, u32[]{:S(2)}, u32[]{:S(2)}) %collective-permute-start.41) | collective-permute-done | bytes 131104 | tf_op jit(solution)/shard_map/ppermute | solution.py:27
  360.2 2.3 collective-permute-start.54
  364.0 66.7 %collective-permute-done.54 = bf16[128,512]{1,0:T(8,128)(2,1)S(1)} collective-permute-done((bf16[128,512]{1,0:T(8,128)(2,1)S(1)}, bf16[128,512]{1,0:T(8,128)(2,1)S(1)}, u32[]{:S(2)}, u32[]{:S(2)}) %collective-permute-start.54) | collective-permute-done | bytes 131104 | tf_op jit(solution)/shard_map/ppermute | solution.py:27
  432.9 2.4 add_convert_fusion.6
  435.3 2.7 shard_map.129
  (222 shorter events, 75.1 us)
Async XLA Ops:
  7.2 139.0 %all-gather.2.cloned.1.call-start = ((), (), s32[]{:S(2)}) async-start(), calls=%async_computation.1 | async-start | bytes 2162688 | tf_op jit(solution)/shard_map/all_gather | solution.py:302
  11.2 70.8 %collective-permute-start.13 = (bf16[128,4096]{1,0:T(8,128)(2,1)S(1)}, bf16[128,4096]{1,0:T(8,128)(2,1)S(1)}, u32[]{:S(2)}, u32[]{:S(2)}) collective-permute-start(bf16[128,4096]{1,0:T(8,128)(2,1)S(1)} %get-tuple-element.15), channel_id=1, source_target_pairs={{0,2},{1,3},{2,0},{3,1},{4,6},{5,7},{6,4},{7,5},{8,10},{9,11},{10,... | collective-permute-start | bytes 3145736 | tf_op jit(solution)/shard_map/ppermute | solution.py:32
  12.9 69.5 %collective-permute-start.14 = (bf16[128,4096]{1,0:T(8,128)(2,1)S(1)}, bf16[128,4096]{1,0:T(8,128)(2,1)}, u32[]{:S(2)}, u32[]{:S(2)}) collective-permute-start(bf16[128,4096]{1,0:T(8,128)(2,1)S(1)} %get-tuple-element.15), channel_id=1, source_target_pairs={{0,1},{1,0},{2,3},{3,2},{4,5},{5,4},{6,7},{7,6},{8,9},{9,8},{10,11... | collective-permute-start | bytes 3145736 | tf_op jit(solution)/shard_map/ppermute | solution.py:32
  12.9 30.0 %collective-permute-start.16 = (bf16[128,512]{1,0:T(8,128)(2,1)}, bf16[128,512]{1,0:T(8,128)(2,1)S(1)}, u32[]{:S(2)}, u32[]{:S(2)}) collective-permute-start(bf16[128,512]{1,0:T(8,128)(2,1)} %param.11), channel_id=1, source_target_pairs={{0,4},{4,0},{8,12},{12,8},{16,20},{20,16},{24,28},{28,24},{32,36},... | collective-permute-start | bytes 393224 | tf_op jit(solution)/shard_map/ppermute | solution.py:27
  15.6 31.8 %collective-permute-start.3 = (bf16[128,512]{1,0:T(8,128)(2,1)}, bf16[128,512]{1,0:T(8,128)(2,1)}, u32[]{:S(2)}, u32[]{:S(2)}) collective-permute-start(bf16[128,512]{1,0:T(8,128)(2,1)} %param.9), channel_id=1, source_target_pairs={{0,4},{4,0},{8,12},{12,8},{16,20},{20,16},{24,28},{28,24},{32,36},... | collective-permute-start | bytes 393224 | tf_op jit(solution)/shard_map/ppermute | solution.py:27
  17.9 421.6 %reduce-scatter.2.cloned.1.call-start = ((), (), s32[]{:S(2)}) async-start(), calls=%async_computation.2 | async-start | bytes 2162688 | tf_op jit(solution)/shard_map/reduce_scatter | solution.py:343
  47.3 8.4 %collective-permute-start.17 = (bf16[256,512]{1,0:T(8,128)(2,1)}, bf16[256,512]{1,0:T(8,128)(2,1)}, u32[]{:S(2)}, u32[]{:S(2)}) collective-permute-start(bf16[256,512]{1,0:T(8,128)(2,1)} %get-tuple-element.63), channel_id=1, source_target_pairs={{0,8},{4,12},{8,0},{12,4},{16,24},{20,28},{24,16},{28,20},{32,40},... | collective-permute-start | bytes 786440 | tf_op jit(solution)/shard_map/ppermute | solution.py:27
  49.1 10.0 %collective-permute-start.4 = (bf16[256,512]{1,0:T(8,128)(2,1)}, bf16[256,512]{1,0:T(8,128)(2,1)}, u32[]{:S(2)}, u32[]{:S(2)}) collective-permute-start(bf16[256,512]{1,0:T(8,128)(2,1)} %get-tuple-element.73), channel_id=1, source_target_pairs={{0,32},{4,36},{8,40},{12,44},{16,48},{20,52},{24,56},{28,60},{32,0... | collective-permute-start | bytes 786440 | tf_op jit(solution)/shard_map/ppermute | solution.py:27
  51.5 13.6 %collective-permute-start.5 = (bf16[256,512]{1,0:T(8,128)(2,1)}, bf16[256,512]{1,0:T(8,128)(2,1)}, u32[]{:S(2)}, u32[]{:S(2)}) collective-permute-start(bf16[256,512]{1,0:T(8,128)(2,1)} %get-tuple-element.73), channel_id=1, source_target_pairs={{0,96},{4,100},{8,104},{12,108},{16,112},{20,116},{24,120},{28,124... | collective-permute-start | bytes 786440 | tf_op jit(solution)/shard_map/ppermute | solution.py:27
  55.7 10.4 %collective-permute-start.19 = (bf16[128,512]{1,0:T(8,128)(2,1)S(1)}, bf16[128,512]{1,0:T(8,128)(2,1)S(1)}, u32[]{:S(2)}, u32[]{:S(2)}) collective-permute-start(bf16[128,512]{1,0:T(8,128)(2,1)S(1)} %slice.267), channel_id=1, source_target_pairs={{0,8},{4,12},{8,0},{12,4},{16,24},{20,28},{24,16},{28,20},{32,40},... | collective-permute-start | bytes 393224 | tf_op jit(solution)/shard_map/ppermute | solution.py:27
  65.1 30.7 %collective-permute-start = (bf16[128,4096]{1,0:T(8,128)(2,1)S(1)}, bf16[128,4096]{1,0:T(8,128)(2,1)S(1)}, u32[]{:S(2)}, u32[]{:S(2)}) collective-permute-start(bf16[128,4096]{1,0:T(8,128)(2,1)S(1)} %get-tuple-element.14), channel_id=1, source_target_pairs={{0,2},{1,3},{2,0},{3,1},{4,6},{5,7},{6,4},{7,5},{8,10},{9,11},{10,... | collective-permute-start | bytes 3145736 | tf_op jit(solution)/shard_map/ppermute | solution.py:32
  67.0 39.2 %collective-permute-start.1 = (bf16[128,4096]{1,0:T(8,128)(2,1)S(1)}, bf16[128,4096]{1,0:T(8,128)(2,1)S(1)}, u32[]{:S(2)}, u32[]{:S(2)}) collective-permute-start(bf16[128,4096]{1,0:T(8,128)(2,1)S(1)} %get-tuple-element.14), channel_id=1, source_target_pairs={{0,1},{1,0},{2,3},{3,2},{4,5},{5,4},{6,7},{7,6},{8,9},{9,8},{10,11... | collective-permute-start | bytes 3145736 | tf_op jit(solution)/shard_map/ppermute | solution.py:32
  79.5 24.9 %collective-permute-start.22 = (bf16[1024,512]{1,0:T(8,128)(2,1)}, bf16[1024,512]{1,0:T(8,128)(2,1)S(1)}, u32[]{:S(2)}, u32[]{:S(2)}) collective-permute-start(bf16[1024,512]{1,0:T(8,128)(2,1)} %get-tuple-element.49), channel_id=1, source_target_pairs={{0,96},{4,100},{8,104},{12,108},{16,112},{20,116},{24,120},{28,124... | collective-permute-start | bytes 3145736 | tf_op jit(solution)/shard_map/ppermute | solution.py:27
  82.0 24.0 %collective-permute-start.21 = (bf16[1024,512]{1,0:T(8,128)(2,1)}, bf16[1024,512]{1,0:T(8,128)(2,1)S(1)}, u32[]{:S(2)}, u32[]{:S(2)}) collective-permute-start(bf16[1024,512]{1,0:T(8,128)(2,1)} %get-tuple-element.49), channel_id=1, source_target_pairs={{0,32},{4,36},{8,40},{12,44},{16,48},{20,52},{24,56},{28,60},{32,0... | collective-permute-start | bytes 3145736 | tf_op jit(solution)/shard_map/ppermute | solution.py:27
  82.4 25.2 %collective-permute-start.9 = (bf16[1024,512]{1,0:T(8,128)(2,1)}, bf16[1024,512]{1,0:T(8,128)(2,1)S(1)}, u32[]{:S(2)}, u32[]{:S(2)}) collective-permute-start(bf16[1024,512]{1,0:T(8,128)(2,1)} %get-tuple-element.53), channel_id=1, source_target_pairs={{0,24},{4,28},{8,16},{12,20},{16,8},{20,12},{24,0},{28,4},{32,56},... | collective-permute-start | bytes 3145736 | tf_op jit(solution)/shard_map/ppermute | solution.py:27
  95.8 17.2 %collective-permute-start.26 = (bf16[512,896]{1,0:T(8,128)(2,1)}, bf16[512,896]{1,0:T(8,128)(2,1)}, u32[]{:S(2)}, u32[]{:S(2)}) collective-permute-start(bf16[512,896]{1,0:T(8,128)(2,1)} %bitcast.31), channel_id=1, source_target_pairs={{0,2},{1,3},{2,0},{3,1},{4,6},{5,7},{6,4},{7,5},{8,10},{9,11},{10,... | collective-permute-start | bytes 2752520 | tf_op jit(solution)/shard_map/ppermute | solution.py:32
  104.4 19.7 %collective-permute-start.8 = (bf16[1024,512]{1,0:T(8,128)(2,1)S(1)}, bf16[1024,512]{1,0:T(8,128)(2,1)S(1)}, u32[]{:S(2)}, u32[]{:S(2)}) collective-permute-start(bf16[1024,512]{1,0:T(8,128)(2,1)S(1)} %copy-done.20), channel_id=1, source_target_pairs={{0,8},{4,12},{8,0},{12,4},{16,24},{20,28},{24,16},{28,20},{32,40},... | collective-permute-start | bytes 3145736 | tf_op jit(solution)/shard_map/ppermute | solution.py:27
  106.0 20.6 %collective-permute-start.15 = (bf16[128,4096]{1,0:T(8,128)(2,1)S(1)}, bf16[128,4096]{1,0:T(8,128)(2,1)S(1)}, u32[]{:S(2)}, u32[]{:S(2)}) collective-permute-start(bf16[128,4096]{1,0:T(8,128)(2,1)S(1)} %collective-permute-done.13), channel_id=1, source_target_pairs={{0,1},{1,0},{2,3},{3,2},{4,5},{5,4},{6,7},{7,6},{8,9},{9,8},{10,11... | collective-permute-start | bytes 3145736 | tf_op jit(solution)/shard_map/ppermute | solution.py:32
  106.2 18.0 %collective-permute-start.23 = (bf16[512,512]{1,0:T(8,128)(2,1)S(1)}, bf16[512,512]{1,0:T(8,128)(2,1)S(1)}, u32[]{:S(2)}, u32[]{:S(2)}) collective-permute-start(bf16[512,512]{1,0:T(8,128)(2,1)S(1)} %slice.269), channel_id=1, source_target_pairs={{0,32},{4,36},{8,40},{12,44},{16,48},{20,52},{24,56},{28,60},{32,0... | collective-permute-start | bytes 1572872 | tf_op jit(solution)/shard_map/ppermute | solution.py:27
  107.6 17.3 %collective-permute-start.24 = (bf16[512,512]{1,0:T(8,128)(2,1)S(1)}, bf16[512,512]{1,0:T(8,128)(2,1)S(1)}, u32[]{:S(2)}, u32[]{:S(2)}) collective-permute-start(bf16[512,512]{1,0:T(8,128)(2,1)S(1)} %slice.270), channel_id=1, source_target_pairs={{0,96},{4,100},{8,104},{12,108},{16,112},{20,116},{24,120},{28,124... | collective-permute-start | bytes 1572872 | tf_op jit(solution)/shard_map/ppermute | solution.py:27
  113.0 36.9 %collective-permute-start.27 = (bf16[512,896]{1,0:T(8,128)(2,1)S(1)}, bf16[512,896]{1,0:T(8,128)(2,1)}, u32[]{:S(2)}, u32[]{:S(2)}) collective-permute-start(bf16[512,896]{1,0:T(8,128)(2,1)S(1)} %bitcast.32), channel_id=1, source_target_pairs={{0,1},{1,0},{2,3},{3,2},{4,5},{5,4},{6,7},{7,6},{8,9},{9,8},{10,11... | collective-permute-start | bytes 2752520 | tf_op jit(solution)/shard_map/ppermute | solution.py:32
  124.1 25.9 %collective-permute-start.28 = (bf16[512,896]{1,0:T(8,128)(2,1)}, bf16[512,896]{1,0:T(8,128)(2,1)}, u32[]{:S(2)}, u32[]{:S(2)}) collective-permute-start(bf16[512,896]{1,0:T(8,128)(2,1)} %collective-permute-done.26), channel_id=1, source_target_pairs={{0,1},{1,0},{2,3},{3,2},{4,5},{5,4},{6,7},{7,6},{8,9},{9,8},{10,11... | collective-permute-start | bytes 2752520 | tf_op jit(solution)/shard_map/ppermute | solution.py:32
  124.2 17.3 %collective-permute-start.2 = (bf16[128,4096]{1,0:T(8,128)(2,1)S(1)}, bf16[128,4096]{1,0:T(8,128)(2,1)S(1)}, u32[]{:S(2)}, u32[]{:S(2)}) collective-permute-start(bf16[128,4096]{1,0:T(8,128)(2,1)S(1)} %collective-permute-done), channel_id=1, source_target_pairs={{0,1},{1,0},{2,3},{3,2},{4,5},{5,4},{6,7},{7,6},{8,9},{9,8},{10,11... | collective-permute-start | bytes 3145736 | tf_op jit(solution)/shard_map/ppermute | solution.py:32
  124.9 13.9 %collective-permute-start.10 = (bf16[512,512]{1,0:T(8,128)(2,1)S(1)}, bf16[512,512]{1,0:T(8,128)(2,1)S(1)}, u32[]{:S(2)}, u32[]{:S(2)}) collective-permute-start(bf16[512,512]{1,0:T(8,128)(2,1)S(1)} %slice.265), channel_id=1, source_target_pairs={{0,8},{4,12},{8,0},{12,4},{16,24},{20,28},{24,16},{28,20},{32,40},... | collective-permute-start | bytes 1572872 | tf_op jit(solution)/shard_map/ppermute | solution.py:27
  126.6 14.9 %collective-permute-start.11 = (bf16[512,512]{1,0:T(8,128)(2,1)S(1)}, bf16[512,512]{1,0:T(8,128)(2,1)S(1)}, u32[]{:S(2)}, u32[]{:S(2)}) collective-permute-start(bf16[512,512]{1,0:T(8,128)(2,1)S(1)} %slice.266), channel_id=1, source_target_pairs={{0,24},{4,28},{8,16},{12,20},{16,8},{20,12},{24,0},{28,4},{32,56},... | collective-permute-start | bytes 1572872 | tf_op jit(solution)/shard_map/ppermute | solution.py:27
  138.8 18.1 %collective-permute-start.25 = (bf16[64,512]{1,0:T(8,128)(2,1)S(1)}, bf16[64,512]{1,0:T(8,128)(2,1)S(1)}, u32[]{:S(2)}, u32[]{:S(2)}) collective-permute-start(bf16[64,512]{1,0:T(8,128)(2,1)S(1)} %constant_dynamic-slice_fusion), channel_id=1, source_target_pairs={{4,0},{8,4},{12,8},{20,16},{24,20},{28,24},{36,32},{40,36},{44,40}... | collective-permute-start | bytes 196616 | tf_op jit(solution)/shard_map/ppermute | solution.py:329
  144.9 12.0 %collective-permute-start.12 = (bf16[64,512]{1,0:T(8,128)(2,1)S(1)}, bf16[64,512]{1,0:T(8,128)(2,1)S(1)}, u32[]{:S(2)}, u32[]{:S(2)}) collective-permute-start(bf16[64,512]{1,0:T(8,128)(2,1)S(1)} %constant_dynamic-slice_fusion.1), channel_id=1, source_target_pairs={{4,0},{8,4},{12,8},{20,16},{24,20},{28,24},{36,32},{40,36},{44,40}... | collective-permute-start | bytes 196616 | tf_op jit(solution)/shard_map/ppermute | solution.py:329
  174.9 27.6 %collective-permute-start.29 = (bf16[64,512]{1,0:T(8,128)(2,1)S(1)}, bf16[64,512]{1,0:T(8,128)(2,1)S(1)}, u32[]{:S(2)}, u32[]{:S(2)}) collective-permute-start(bf16[64,512]{1,0:T(8,128)(2,1)S(1)} %get-tuple-element.17), channel_id=1, source_target_pairs={{0,4},{4,8},{8,12},{16,20},{20,24},{24,28},{32,36},{36,40},{40,44}... | collective-permute-start | bytes 196616 | tf_op jit(solution)/shard_map/ppermute | solution.py:336
  181.0 30.9 %collective-permute-start.32 = (bf16[64,512]{1,0:T(8,128)(2,1)S(1)}, bf16[64,512]{1,0:T(8,128)(2,1)S(1)}, u32[]{:S(2)}, u32[]{:S(2)}) collective-permute-start(bf16[64,512]{1,0:T(8,128)(2,1)S(1)} %get-tuple-element.19), channel_id=1, source_target_pairs={{0,4},{4,8},{8,12},{16,20},{20,24},{24,28},{32,36},{36,40},{40,44}... | collective-permute-start | bytes 196616 | tf_op jit(solution)/shard_map/ppermute | solution.py:336
  195.0 156.8 %collective-permute-start.35 = (bf16[1024,896]{1,0:T(8,128)(2,1)}, bf16[1024,896]{1,0:T(8,128)(2,1)}, u32[]{:S(2)}, u32[]{:S(2)}) collective-permute-start(bf16[1024,896]{1,0:T(8,128)(2,1)} %slice.282), channel_id=1, source_target_pairs={{0,1},{1,0},{2,3},{3,2},{4,5},{5,4},{6,7},{7,6},{8,9},{9,8},{10,11... | collective-permute-start | bytes 5505032 | tf_op jit(solution)/shard_map/ppermute | solution.py:32
  208.5 93.1 %collective-permute-start.46 = (bf16[512,512]{1,0:T(8,128)(2,1)}, bf16[512,512]{1,0:T(8,128)(2,1)}, u32[]{:S(2)}, u32[]{:S(2)}) collective-permute-start(bf16[512,512]{1,0:T(8,128)(2,1)} %get-tuple-element.27), channel_id=1, source_target_pairs={{0,96},{4,100},{8,104},{12,108},{16,112},{20,116},{24,120},{28,124... | collective-permute-start | bytes 1572872 | tf_op jit(solution)/shard_map/ppermute | solution.py:27
  210.8 90.7 %collective-permute-start.48 = (bf16[512,512]{1,0:T(8,128)(2,1)}, bf16[512,512]{1,0:T(8,128)(2,1)}, u32[]{:S(2)}, u32[]{:S(2)}) collective-permute-start(bf16[512,512]{1,0:T(8,128)(2,1)} %get-tuple-element.28), channel_id=1, source_target_pairs={{0,32},{4,36},{8,40},{12,44},{16,48},{20,52},{24,56},{28,60},{32,0... | collective-permute-start | bytes 1572872 | tf_op jit(solution)/shard_map/ppermute | solution.py:27
  217.8 89.8 %collective-permute-start.37 = (bf16[512,512]{1,0:T(8,128)(2,1)}, bf16[512,512]{1,0:T(8,128)(2,1)}, u32[]{:S(2)}, u32[]{:S(2)}) collective-permute-start(bf16[512,512]{1,0:T(8,128)(2,1)} %get-tuple-element.33), channel_id=1, source_target_pairs={{0,24},{4,28},{8,16},{12,20},{16,8},{20,12},{24,0},{28,4},{32,56},... | collective-permute-start | bytes 1572872 | tf_op jit(solution)/shard_map/ppermute | solution.py:27
  219.5 88.2 %collective-permute-start.39 = (bf16[512,512]{1,0:T(8,128)(2,1)}, bf16[512,512]{1,0:T(8,128)(2,1)}, u32[]{:S(2)}, u32[]{:S(2)}) collective-permute-start(bf16[512,512]{1,0:T(8,128)(2,1)} %get-tuple-element.34), channel_id=1, source_target_pairs={{0,8},{4,12},{8,0},{12,4},{16,24},{20,28},{24,16},{28,20},{32,40},... | collective-permute-start | bytes 1572872 | tf_op jit(solution)/shard_map/ppermute | solution.py:27
  305.0 26.5 %collective-permute-start.47 = (bf16[1024,512]{1,0:T(8,128)(2,1)S(1)}, bf16[1024,512]{1,0:T(8,128)(2,1)S(1)}, u32[]{:S(2)}, u32[]{:S(2)}) collective-permute-start(bf16[1024,512]{1,0:T(8,128)(2,1)S(1)} %pad_maximum_fusion.3), channel_id=1, source_target_pairs={{0,32},{4,36},{8,40},{12,44},{16,48},{20,52},{24,56},{28,60},{32,0... | collective-permute-start | bytes 3145736 | tf_op jit(solution)/shard_map/ppermute | solution.py:27
  306.3 29.0 %collective-permute-start.49 = (bf16[1024,512]{1,0:T(8,128)(2,1)S(1)}, bf16[1024,512]{1,0:T(8,128)(2,1)S(1)}, u32[]{:S(2)}, u32[]{:S(2)}) collective-permute-start(bf16[1024,512]{1,0:T(8,128)(2,1)S(1)} %pad_maximum_fusion.4), channel_id=1, source_target_pairs={{0,96},{4,100},{8,104},{12,108},{16,112},{20,116},{24,120},{28,124... | collective-permute-start | bytes 3145736 | tf_op jit(solution)/shard_map/ppermute | solution.py:27
  309.2 26.6 %collective-permute-start.38 = (bf16[1024,512]{1,0:T(8,128)(2,1)S(1)}, bf16[1024,512]{1,0:T(8,128)(2,1)S(1)}, u32[]{:S(2)}, u32[]{:S(2)}) collective-permute-start(bf16[1024,512]{1,0:T(8,128)(2,1)S(1)} %pad_maximum_fusion.1), channel_id=1, source_target_pairs={{0,8},{4,12},{8,0},{12,4},{16,24},{20,28},{24,16},{28,20},{32,40},... | collective-permute-start | bytes 3145736 | tf_op jit(solution)/shard_map/ppermute | solution.py:27
  310.3 28.6 %collective-permute-start.40 = (bf16[1024,512]{1,0:T(8,128)(2,1)S(1)}, bf16[1024,512]{1,0:T(8,128)(2,1)S(1)}, u32[]{:S(2)}, u32[]{:S(2)}) collective-permute-start(bf16[1024,512]{1,0:T(8,128)(2,1)S(1)} %pad_maximum_fusion.2), channel_id=1, source_target_pairs={{0,24},{4,28},{8,16},{12,20},{16,8},{20,12},{24,0},{28,4},{32,56},... | collective-permute-start | bytes 3145736 | tf_op jit(solution)/shard_map/ppermute | solution.py:27
  331.4 22.5 %collective-permute-start.33 = (bf16[256,4096]{1,0:T(8,128)(2,1)}, bf16[256,4096]{1,0:T(8,128)(2,1)S(1)}, u32[]{:S(2)}, u32[]{:S(2)}) collective-permute-start(bf16[256,4096]{1,0:T(8,128)(2,1)} %slice.277), channel_id=1, source_target_pairs={{0,1},{1,0},{2,3},{3,2},{4,5},{5,4},{6,7},{7,6},{8,9},{9,8},{10,11... | collective-permute-start | bytes 6291464 | tf_op jit(solution)/shard_map/ppermute | solution.py:32
  335.3 20.7 %collective-permute-start.30 = (bf16[256,4096]{1,0:T(8,128)(2,1)S(1)}, bf16[256,4096]{1,0:T(8,128)(2,1)S(1)}, u32[]{:S(2)}, u32[]{:S(2)}) collective-permute-start(bf16[256,4096]{1,0:T(8,128)(2,1)S(1)} %slice.272), channel_id=1, source_target_pairs={{0,1},{1,0},{2,3},{3,2},{4,5},{5,4},{6,7},{7,6},{8,9},{9,8},{10,11... | collective-permute-start | bytes 6291464 | tf_op jit(solution)/shard_map/ppermute | solution.py:32
  350.4 8.8 %collective-permute-start.53 = (bf16[256,512]{1,0:T(8,128)(2,1)S(1)}, bf16[256,512]{1,0:T(8,128)(2,1)S(1)}, u32[]{:S(2)}, u32[]{:S(2)}) collective-permute-start(bf16[256,512]{1,0:T(8,128)(2,1)S(1)} %pad_maximum_fusion.10), channel_id=1, source_target_pairs={{0,24},{4,28},{8,16},{12,20},{16,8},{20,12},{24,0},{28,4},{32,56},... | collective-permute-start | bytes 786440 | tf_op jit(solution)/shard_map/ppermute | solution.py:27
  351.8 8.4 %collective-permute-start.42 = (bf16[256,512]{1,0:T(8,128)(2,1)S(1)}, bf16[256,512]{1,0:T(8,128)(2,1)S(1)}, u32[]{:S(2)}, u32[]{:S(2)}) collective-permute-start(bf16[256,512]{1,0:T(8,128)(2,1)S(1)} %pad_maximum_fusion.7), channel_id=1, source_target_pairs={{0,32},{4,36},{8,40},{12,44},{16,48},{20,52},{24,56},{28,60},{32,0... | collective-permute-start | bytes 786440 | tf_op jit(solution)/shard_map/ppermute | solution.py:27
  353.9 9.3 %collective-permute-start.44 = (bf16[256,512]{1,0:T(8,128)(2,1)S(1)}, bf16[256,512]{1,0:T(8,128)(2,1)S(1)}, u32[]{:S(2)}, u32[]{:S(2)}) collective-permute-start(bf16[256,512]{1,0:T(8,128)(2,1)S(1)} %pad_maximum_fusion.8), channel_id=1, source_target_pairs={{0,96},{4,100},{8,104},{12,108},{16,112},{20,116},{24,120},{28,124... | collective-permute-start | bytes 786440 | tf_op jit(solution)/shard_map/ppermute | solution.py:27
  356.0 76.8 %collective-permute-start.36 = (bf16[512,896]{1,0:T(8,128)(2,1)S(1)}, bf16[512,896]{1,0:T(8,128)(2,1)S(1)}, u32[]{:S(2)}, u32[]{:S(2)}) collective-permute-start(bf16[512,896]{1,0:T(8,128)(2,1)S(1)} %add_convert_fusion.7), channel_id=1, source_target_pairs={{0,2},{1,3},{2,0},{3,1},{4,6},{5,7},{6,4},{7,5},{8,10},{9,11},{10,... | collective-permute-start | bytes 2752520 | tf_op jit(solution)/shard_map/ppermute | solution.py:32
  357.9 77.4 %collective-permute-start.34 = (bf16[128,4096]{1,0:T(8,128)(2,1)S(1)}, bf16[128,4096]{1,0:T(8,128)(2,1)S(1)}, u32[]{:S(2)}, u32[]{:S(2)}) collective-permute-start(bf16[128,4096]{1,0:T(8,128)(2,1)S(1)} %get-tuple-element.21), channel_id=1, source_target_pairs={{0,2},{1,3},{2,0},{3,1},{4,6},{5,7},{6,4},{7,5},{8,10},{9,11},{10,... | collective-permute-start | bytes 3145736 | tf_op jit(solution)/shard_map/ppermute | solution.py:32
  359.2 78.8 %collective-permute-start.31 = (bf16[128,4096]{1,0:T(8,128)(2,1)S(1)}, bf16[128,4096]{1,0:T(8,128)(2,1)S(1)}, u32[]{:S(2)}, u32[]{:S(2)}) collective-permute-start(bf16[128,4096]{1,0:T(8,128)(2,1)S(1)} %get-tuple-element.23), channel_id=1, source_target_pairs={{0,2},{1,3},{2,0},{3,1},{4,6},{5,7},{6,4},{7,5},{8,10},{9,11},{10,... | collective-permute-start | bytes 3145736 | tf_op jit(solution)/shard_map/ppermute | solution.py:32
  360.2 70.5 %collective-permute-start.54 = (bf16[128,512]{1,0:T(8,128)(2,1)S(1)}, bf16[128,512]{1,0:T(8,128)(2,1)S(1)}, u32[]{:S(2)}, u32[]{:S(2)}) collective-permute-start(bf16[128,512]{1,0:T(8,128)(2,1)S(1)} %slice.317), channel_id=1, source_target_pairs={{0,4},{4,0},{8,12},{12,8},{16,20},{20,16},{24,28},{28,24},{32,36},... | collective-permute-start | bytes 393224 | tf_op jit(solution)/shard_map/ppermute | solution.py:27
  363.3 68.8 %collective-permute-start.45 = (bf16[128,512]{1,0:T(8,128)(2,1)S(1)}, bf16[128,512]{1,0:T(8,128)(2,1)S(1)}, u32[]{:S(2)}, u32[]{:S(2)}) collective-permute-start(bf16[128,512]{1,0:T(8,128)(2,1)S(1)} %slice.301), channel_id=1, source_target_pairs={{0,4},{4,0},{8,12},{12,8},{16,20},{20,16},{24,28},{28,24},{32,36},... | collective-permute-start | bytes 393224 | tf_op jit(solution)/shard_map/ppermute | solution.py:27
  (38 other events, 564.9 us)
Sparse Core Ops, SparseCore 0:
  18.0 79.9 all-gather.1
  202.7 195.4 reduce-scatter.1
